TPU v7x, 32 devices: a whole 2x2x4 slice. The times are simulated.
32 devices in a mesh: dp: 4 (over x, core), tensor: 8 (over z, y).
Axes of the slice: x: 2, y: 2, z: 4, core: 2. Of those that a mesh axis runs over, the one named last changes fastest.
Arguments:
- old_m_codes: bfloat16 [4096, 2048], P(('dp', 'tensor')), may hold values from -1 to 1
- old_m_scale: float32 [4096], P(('dp', 'tensor')), may hold values from 0.3 to 3
- old_v_codes: bfloat16 [4096, 2048], P(('dp', 'tensor')), may hold values from 0.019897461 to 1
- old_v_scale: float32 [4096], P(('dp', 'tensor')), may hold values from 1 to 10
- block_target: int32 [4096], replicated, may hold values from 0 to 4095, as said below
- new_offset: int32 [32], P(('dp', 'tensor')), may hold values from 128 to 1920, as said below
- grad_part: bfloat16 [4, 8, 512, 2048], P('dp', 'tensor'), may hold values from -6 to 6
- master_weight: float32 [8, 512, 2048], P('tensor', 'dp'), may hold values from -6 to 6
Outputs:
- new_m_codes: bfloat16 [8, 512, 2048], P('tensor', 'dp')
- new_m_scale: float32 [32, 129], P(('dp', 'tensor'))
- new_v_codes: bfloat16 [8, 512, 2048], P('tensor', 'dp')
- new_v_scale: float32 [32, 129], P(('dp', 'tensor'))
- adam_update: float32 [8, 512, 2048], P('tensor', 'dp')
- new_weight: bfloat16 [8, 512, 2048], P('tensor', 'dp')
Inputs may be any that keep to these rules, and one draw needn't show every extreme that they name: block_target is a bijection of the old blocks onto the new ones. Device n along dp+tensor holds old blocks n * 128 to (n+1) * 128 - 1. At most 8 old blocks of one device go to one new owner, and exactly 8 for some pairs. `new_offset`: multiples of 128.
All inputs are finite; a program needn't handle non-finite values. Where the computation divides by a largest or mean magnitude, that divisor is 1e-20 or more.
Results may differ from a plain program's by a relative error of at most 0.013.
Values may be sent and summed in bfloat16 or wider, within the bound.
A program may use at most 128 MiB of HBM per device.

v0:
```python
import jax
import jax.numpy as jnp
from jax import lax
from jax.sharding import PartitionSpec as P

FIRST_DECAY = 0.9
SECOND_DECAY = 0.95
FIRST_CORRECTION = 1.0 - 0.9**40
SECOND_CORRECTION = 1.0 - 0.95**40
ADAM_EPSILON = 1e-08
WEIGHT_DECAY = 0.1
LEARN_RATE = 6e-05


def requantize(flat, offset, held, size):
    start = size - offset
    padded = lax.dynamic_update_slice(jnp.zeros(((held + 1) * size,), jnp.float32), flat, (start,))
    blocks = padded.reshape(held + 1, size)
    scales = jnp.max(jnp.abs(blocks), axis=1) + 1e-06
    codes = (blocks / scales[:, None]).reshape(-1)
    return (lax.dynamic_slice(codes, (start,), (held * size,)).astype(jnp.bfloat16), scales)


def local(
    old_m_codes,
    old_m_scale,
    old_v_codes,
    old_v_scale,
    block_target,
    new_offset,
    grad_part,
    master_weight,
):
    dp_count = lax.axis_size("dp")
    tp_count = lax.axis_size("tensor")
    owners = dp_count * tp_count
    held = old_m_codes.shape[0]
    size = old_m_codes.shape[1]
    capacity = max(2, 2 * held // owners)
    myself = lax.axis_index("dp") * tp_count + lax.axis_index("tensor")
    columns = jnp.arange(held, dtype=jnp.int32)
    targets = lax.dynamic_slice_in_dim(block_target, myself * held, held)
    owner_of = targets // held
    before = (owner_of[:, None] == owner_of[None, :]) & (columns[None, :] < columns[:, None])
    place = owner_of * capacity + jnp.sum(before, axis=1, dtype=jnp.int32)
    total = block_target.shape[0]
    all_owner = (block_target // held).reshape(owners, held)
    anchor = jnp.zeros_like(block_target).at[block_target].set(jnp.arange(total, dtype=jnp.int32))
    mine = lax.dynamic_slice_in_dim(anchor, myself * held, held)
    source = mine // held
    within = mine % held
    source_rows = all_owner[source]
    earlier = (source_rows == myself) & (columns[None, :] < within[:, None])
    pick = source * capacity + jnp.sum(earlier, axis=1, dtype=jnp.int32)
    moments = jnp.stack(
        [
            old_m_codes.astype(jnp.float32) * old_m_scale[:, None],
            old_v_codes.astype(jnp.float32) * old_v_scale[:, None],
        ],
        1,
    )
    outgoing = jnp.zeros((owners * capacity, 2, size), jnp.float32).at[place].set(moments)
    arrived = lax.all_to_all(
        outgoing.reshape(owners, capacity, 2, size),
        ("dp", "tensor"),
        split_axis=0,
        concat_axis=0,
        tiled=True,
    )
    placed = arrived.reshape(owners * capacity, 2, size)[pick]
    m_prev = placed[:, 0]
    v_prev = placed[:, 1]
    grad = lax.psum_scatter(
        grad_part[0, 0].astype(jnp.float32).astype(jnp.bfloat16),
        "dp",
        scatter_dimension=0,
        tiled=True,
    ).astype(jnp.float32)
    master = master_weight[0]
    m_next = FIRST_DECAY * m_prev + (1.0 - FIRST_DECAY) * grad
    v_next = SECOND_DECAY * v_prev + (1.0 - SECOND_DECAY) * grad * grad
    adam_update = (
        m_next / FIRST_CORRECTION / (jnp.sqrt(v_next / SECOND_CORRECTION) + ADAM_EPSILON)
        + WEIGHT_DECAY * master
    )
    new_weight = (master - LEARN_RATE * adam_update).astype(jnp.bfloat16)
    offset = new_offset[0]
    m_codes, m_scale = requantize(m_next.reshape(-1), offset, held, size)
    v_codes, v_scale = requantize(v_next.reshape(-1), offset, held, size)
    return (
        m_codes.reshape(1, held, size),
        m_scale.reshape(1, held + 1),
        v_codes.reshape(1, held, size),
        v_scale.reshape(1, held + 1),
        adam_update.reshape(1, held, size),
        new_weight.reshape(1, held, size),
    )


def solution(mesh):
    return jax.shard_map(
        local,
        mesh=mesh,
        in_specs=(
            P(("dp", "tensor"), None),
            P(("dp", "tensor")),
            P(("dp", "tensor"), None),
            P(("dp", "tensor")),
            P(),
            P(("dp", "tensor")),
            P("dp", "tensor", None, None),
            P("tensor", "dp", None),
        ),
        out_specs=(
            P("tensor", "dp", None),
            P(("dp", "tensor"), None),
            P("tensor", "dp", None),
            P(("dp", "tensor"), None),
            P("tensor", "dp", None),
            P("tensor", "dp", None),
        ),
        check_vma=False,
    )
```

profile of v0, /device:TPU:0, one launch (start us, length us, event | category | flops | bytes accessed | tf_op | source)
XLA Modules:
  0.0 191.3 jit_solution(2062092496043543079)
XLA Ops:
  7.2 0.7 add_select_fusion.1
  7.9 15.5 %scatter_custom_fusion.1 = s32[4096]{0:T(1024)S(1)} fusion(s32[4096]{0:T(1024)S(1)} %get-tuple-element.16, s32[4096]{0:T(1024)S(1)} %iota.10, s32[]{:T(128)} %constant.77.clone.1), kind=kCustom, calls=%fused_computation.40 | custom fusion | bytes 16388 | tf_op jit(solution)/shard_map/scatter | solution.py:48
  23.5 0.1 and_select_fusion
  23.5 0.8 compare_select_fusion.1
  24.3 0.2 convert_reduce_fusion.1
  24.5 1.4 multiply_bitcast_fusion
  25.9 0.2 pad_maximum_fusion
  26.2 1.6 copy.16
  27.8 4.1 %broadcast_in_dim.10 = f32[256,2,2048]{2,1,0:T(2,128)} broadcast(f32[]{:T(128)} %constant.72.clone.1), dimensions={} | broadcast | bytes 4194308 | tf_op jit(solution)/shard_map/broadcast_in_dim | solution.py:62
  31.9 15.7 %scatter_fusion = f32[256,2,2048]{2,1,0:T(2,128)} fusion(f32[256,2,2048]{2,1,0:T(2,128)} %broadcast_in_dim.10, s32[128]{0:T(128)S(1)} %compare_select_fusion.2, f32[128,2,2048]{2,1,0:T(2,128)S(1)} %copy.16), kind=kCustom, calls=%fused_computation.2 | custom fusion | bytes 6291968 | tf_op jit(solution)/shard_map/scatter | solution.py:62
  47.6 7.5 %all-to-all-start = ((f32[32,8,2,2048]{3,2,1,0:T(2,128)}), f32[32,8,2,2048]{3,2,1,0:T(2,128)}, u32[]{:S(2)}, u32[]{:S(2)}) async-start(f32[32,8,2,2048]{3,2,1,0:T(2,128)} %bitcast.48), calls=%async_computation | async-start | bytes 8388608 | tf_op jit(solution)/shard_map/all_to_all | solution.py:63
  55.1 0.2 reduce-scatter.2.cloned.1.call-start
  55.3 0.5 reduce-scatter.2.cloned.1.call-update
  56.5 0.6 gather_fusion
  57.1 0.2 convert_reduce_fusion
  57.3 93.8 %all-to-all-done = f32[32,8,2,2048]{3,2,1,0:T(2,128)} async-done(((f32[32,8,2,2048]{3,2,1,0:T(2,128)}), f32[32,8,2,2048]{3,2,1,0:T(2,128)}, u32[]{:S(2)}, u32[]{:S(2)}) %all-to-all-start) | async-done | bytes 4194336 | tf_op jit(solution)/shard_map/all_to_all | solution.py:63
  151.1 5.0 %gather_fusion.1 = f32[128,2,2048]{2,1,0:T(2,128)S(1)} fusion(f32[256,2,2048]{2,1,0:T(2,128)} %bitcast.3, s32[1024]{0:T(1024)S(1)} %pad_clamp_fusion), kind=kCustom, calls=%fused_computation.1 | custom fusion | bytes 4194816 | tf_op jit(solution)/shard_map/gather | solution.py:70
  156.1 2.7 %fusion.18 = (f32[128,1,2048]{2,1,0:T(1,128)S(1)}, f32[128,1,2048]{2,1,0:T(1,128)}) fusion(f32[128,2,2048]{2,1,0:T(2,128)S(1)} %gather_fusion.1), kind=kLoop, calls=%fused_computation.58 | loop fusion | flops 262144 | bytes 4194304 | tf_op jit(solution)/shard_map/slice | solution.py:72
  158.8 0.0 reduce-scatter.2.cloned.1.call-done
  158.8 4.5 %fusion.8 = (bf16[1,128,2048]{2,1,0:T(8,128)(2,1)}, f32[128,2048]{1,0:T(8,128)}, f32[16,16,8,128]{3,2,1,0:T(8,128)}, f32[16,16,8,128]{3,2,1,0:T(8,128)S(1)}) fusion(f32[1,128,2048]{2,1,0:T(8,128)} %param.15, f32[128,1,2048]{2,1,0:T(1,128)S(1)} %get-tuple-element.12, bf16[128,2048]{1,0:T(8,128)(2,1)} %reduce-scatter.2.cloned.1.call-done, ...), kind=kLoop, calls=%fused_computation.23 | loop fusion | flops 4194304 | bytes 7340032 | tf_op jit(solution)/shard_map/reshape | solution.py:96
  163.3 0.2 copy.21
  163.5 0.1 broadcast.78.clone.1
  163.6 7.0 %dynamic_update_slice.7 = f32[264192]{0:T(1024)S(1)} dynamic-update-slice(f32[264192]{0:T(1024)S(1)} %broadcast.78.clone.1, f32[262144]{0:T(1024)S(1)} %bitcast.50, s32[]{:T(128)S(6)} %select_n.51) | dynamic-update-slice | bytes 2097156 | tf_op jit(solution)/shard_map/dynamic_update_slice | solution.py:17
  170.6 0.1 abs.14
  170.7 0.2 abs.15
  170.8 0.1 reduce_max.19
  171.0 0.0 copy-start.1
  171.0 0.1 div.83
  171.1 0.2 div.84
  171.3 0.0 copy-start
  171.3 1.4 fusion.2
  172.7 0.0 copy-done.1
  172.7 2.1 %reshape.92 = bf16[1,128,2048]{2,1,0:T(8,128)(2,1)} reshape(bf16[262144]{0:T(1024)(128)(2,1)} %fusion.2) | data formatting | bytes 1048576 | tf_op jit(solution)/shard_map/reshape | solution.py:93
  174.8 0.0 copy-done
  174.8 0.2 copy.20
  175.0 0.1 broadcast.78.clone
  175.1 7.0 %dynamic_update_slice.6 = f32[264192]{0:T(1024)S(1)} dynamic-update-slice(f32[264192]{0:T(1024)S(1)} %broadcast.78.clone, f32[262144]{0:T(1024)S(1)} %bitcast.49, s32[]{:T(128)S(6)} %select_n.51) | dynamic-update-slice | bytes 2097156 | tf_op jit(solution)/shard_map/dynamic_update_slice | solution.py:17
  182.0 0.1 abs.12
  182.1 0.2 abs.13
  182.3 0.1 reduce_max.18
  182.5 0.0 copy-start.2
  182.5 0.1 div.80
  182.6 0.2 div.81
  182.8 0.6 fusion.3
  183.4 0.0 copy-done.2
  183.4 1.0 reshape.90
  (7 shorter events, 0.0 us)
Async XLA Ops:
  47.6 103.5 %all-to-all-start = ((f32[32,8,2,2048]{3,2,1,0:T(2,128)}), f32[32,8,2,2048]{3,2,1,0:T(2,128)}, u32[]{:S(2)}, u32[]{:S(2)}) async-start(f32[32,8,2,2048]{3,2,1,0:T(2,128)} %bitcast.48), calls=%async_computation | async-start | bytes 8388608 | tf_op jit(solution)/shard_map/all_to_all | solution.py:63
  55.1 103.7 %reduce-scatter.2.cloned.1.call-start = ((), (), s32[]{:S(2)}) async-start(), calls=%async_computation.2 | async-start | bytes 2621440 | tf_op jit(solution)/shard_map/reduce_scatter | solution.py:73
  171.0 1.8 copy-start.1
  171.3 3.5 %copy-start = (f32[16,16,8,128]{3,2,1,0:T(8,128)S(1)}, f32[16,16,8,128]{3,2,1,0:T(8,128)}, u32[]{:S(2)}) copy-start(f32[16,16,8,128]{3,2,1,0:T(8,128)} %get-tuple-element.14) | copy-start | bytes 3145732
  182.5 0.9 copy-start.2
Sparse Core Ops, SparseCore 0:
  58.4 41.4 reduce-scatter.1
where the time goes:
time: 192 us; the launch traced here: 191 us
  waiting for transfers between devices  94.3 us (49%)
  local copies, waits for them, and re-layouts  61 us (32%)
  between operations  14.9 us (8%)
  other arithmetic  13.3 us (7%)
  starting transfers between devices  7.71 us (4%)
    all_to_all x1, waiting for transfers between devices, local(): lax.all_to_all(outgoing.reshape(owners, capacity, 2, size), ('dp', 'tenso...  93.8 us
    scatter x1, local copies, waits for them, and re-layouts, local(): jnp.zeros((owners * capacity, 2, size), jnp.float32).at[place].set(moments)  15.7 us
    scatter x1, local copies, waits for them, and re-layouts, local(): jnp.zeros_like(block_target).at[block_target]  15.5 us
    dynamic_update_slice x2, local copies, waits for them, and re-layouts, requantize(): lax.dynamic_update_slice(jnp.zeros(((held + 1) * size,), jnp.float32), fl...  14 us
    all_to_all x1, starting transfers between devices, local(): lax.all_to_all(outgoing.reshape(owners, capacity, 2, size), ('dp', 'tenso...  7.49 us
    gather x1, local copies, waits for them, and re-layouts, local(): placed = arrived.reshape(owners * capacity, 2, size)[pick]  4.97 us
    reshape x1, other arithmetic, local(): new_weight.reshape(1, held, size)  4.48 us
    broadcast_in_dim x1, local copies, waits for them, and re-layouts, local(): jnp.zeros((owners * capacity, 2, size), jnp.float32).at[place].set(moments)  4.1 us
  transfers between devices with their start and end apart: 2, of which 1 were waited for; matrix products, arithmetic and copies ran while one was open for 4% of the time, Pallas kernels for 0%

commit v1 on v0

v1 whole, which is shorter than its diff:
```python
import functools

import jax
import jax.numpy as jnp
from jax import lax
from jax.experimental import pallas as pl
from jax.experimental.pallas import tpu as pltpu
from jax.sharding import PartitionSpec as P

FIRST_DECAY = 0.9
SECOND_DECAY = 0.95
FIRST_CORRECTION = 1.0 - 0.9**40
SECOND_CORRECTION = 1.0 - 0.95**40
ADAM_EPSILON = 1e-08
WEIGHT_DECAY = 0.1
LEARN_RATE = 6e-05
MESH = pl.DeviceIdType.MESH


def column_of(row, held):
    return jnp.broadcast_to(row, (held, held)).T


def exchange(
    n_dp,
    n_tensor,
    capacity,
    targets_ref,
    m_codes_ref,
    m_scale_ref,
    v_codes_ref,
    v_scale_ref,
    grad_ref,
    arrived_ref,
    grads_ref,
    route_ref,
    outgoing,
    send_sem,
    recv_sem,
    grad_send_sem,
    grad_recv_sem,
    local_sem,
):
    owners = n_dp * n_tensor
    held, size = m_codes_ref.shape
    rows = outgoing.shape[1]
    my_dp = lax.axis_index("dp")
    my_tensor = lax.axis_index("tensor")
    myself = my_dp * n_tensor + my_tensor

    barrier = pltpu.get_barrier_semaphore()

    def greet(step, carry):
        other = lax.rem(myself + step, owners)
        pl.semaphore_signal(
            barrier, inc=1, device_id=(other // n_tensor, lax.rem(other, n_tensor)), device_id_type=MESH
        )
        return carry

    lax.fori_loop(1, owners, greet, 0)

    mine = targets_ref[pl.ds(myself, 1), :]
    owner = (mine // held).astype(jnp.float32)
    owner_col = column_of(owner, held)
    owner_row = jnp.broadcast_to(owner, (held, held))
    down = lax.broadcasted_iota(jnp.int32, (held, held), 0)
    across = lax.broadcasted_iota(jnp.int32, (held, held), 1)
    rank = jnp.sum(
        jnp.where((owner_col == owner_row) & (down < across), 1.0, 0.0), axis=0, keepdims=True
    )
    slot = (owner * rows + rank).astype(jnp.int32)
    slots = jnp.concatenate([slot, slot + capacity], axis=1)
    m_old = m_codes_ref[...].astype(jnp.float32) * column_of(m_scale_ref[...], held)[:, :1]
    v_old = v_codes_ref[...].astype(jnp.float32) * column_of(v_scale_ref[...], held)[:, :1]
    moments = jnp.concatenate([m_old.astype(jnp.bfloat16), v_old.astype(jnp.bfloat16)], axis=0)
    some = 8
    for first in range(0, owners, some):
        place = lax.broadcasted_iota(jnp.int32, (some * rows, 2 * held), 0) + first * rows
        chosen = jnp.where(place == slots, 1.0, 0.0).astype(jnp.bfloat16)
        packed = jnp.dot(chosen, moments, preferred_element_type=jnp.float32)
        outgoing[first : first + some] = packed.astype(jnp.bfloat16).reshape(some, rows, size)

    pl.semaphore_wait(barrier, owners - 1)

    def grad_copy(step):
        other = lax.rem(my_dp + step, n_dp)
        return pltpu.make_async_remote_copy(
            src_ref=grad_ref.at[pl.ds(pl.multiple_of(other * held, held), held)],
            dst_ref=grads_ref.at[my_dp],
            send_sem=grad_send_sem.at[other],
            recv_sem=grad_recv_sem.at[my_dp],
            device_id=(other, my_tensor),
            device_id_type=MESH,
        )

    def grad_arrival(step):
        other = lax.rem(my_dp + step, n_dp)
        return pltpu.make_async_remote_copy(
            src_ref=grad_ref.at[pl.ds(pl.multiple_of(other * held, held), held)],
            dst_ref=grads_ref.at[other],
            send_sem=grad_send_sem.at[other],
            recv_sem=grad_recv_sem.at[other],
            device_id=(other, my_tensor),
            device_id_type=MESH,
        )

    def peer(step):
        tensor_step = lax.rem(step // n_dp + n_tensor // 2, n_tensor)
        dp_step = lax.rem(step, n_dp)
        there = lax.rem(my_dp + dp_step, n_dp)
        across = lax.rem(my_tensor + tensor_step, n_tensor)
        return there, across, there * n_tensor + across, (tensor_step + dp_step) > 0

    def send(step, carry):
        there, across, other, remote = peer(step)

        @pl.when(remote)
        def _():
            pltpu.make_async_remote_copy(
                src_ref=outgoing.at[other],
                dst_ref=arrived_ref.at[myself],
                send_sem=send_sem.at[other],
                recv_sem=recv_sem.at[myself],
                device_id=(there, across),
                device_id_type=MESH,
            ).start()

        return carry

    def finish(step, carry):
        there, across, other, remote = peer(step)

        @pl.when(remote)
        def _():
            copy = pltpu.make_async_remote_copy(
                src_ref=outgoing.at[other],
                dst_ref=arrived_ref.at[other],
                send_sem=send_sem.at[other],
                recv_sem=recv_sem.at[other],
                device_id=(there, across),
                device_id_type=MESH,
            )
            copy.wait_send()
            copy.wait_recv()

        return carry

    lax.fori_loop(0, owners, send, 0)
    for step in range(1, n_dp):
        grad_copy(step).start()
    own_grad = pltpu.make_async_copy(
        grad_ref.at[pl.ds(pl.multiple_of(my_dp * held, held), held)], grads_ref.at[my_dp], local_sem.at[0]
    )
    own_grad.start()
    own_slots = pltpu.make_async_copy(outgoing.at[myself], arrived_ref.at[myself], local_sem.at[1])
    own_slots.start()

    targets = targets_ref[...]
    is_mine = jnp.where(targets // held == myself, 1.0, 0.0)
    before = jnp.where(down < across, 1.0, 0.0).astype(jnp.bfloat16)
    ranks = jnp.dot(is_mine.astype(jnp.bfloat16), before, preferred_element_type=jnp.float32)
    ranks = jnp.where(is_mine > 0.0, ranks, -1.0)
    row = lax.rem(targets, held).astype(jnp.float32) + 1.0

    def spread(x):
        return jnp.broadcast_to(x[:, None, :], (owners, rows, held)).reshape(owners * rows, held)

    index = lax.broadcasted_iota(jnp.int32, (owners, rows, held), 1).reshape(owners * rows, held)
    within = jnp.where(index >= capacity, index - capacity, index)
    hit = jnp.where(spread(ranks) == within.astype(jnp.float32), spread(row), 0.0)
    place = jnp.sum(hit, axis=1, keepdims=True).astype(jnp.int32) - 1
    index = index[:, :1]
    place = jnp.where((place >= 0) & (index >= capacity), place + held, place)
    place = jnp.where(index < 2 * capacity, place, -1)
    wanted = lax.broadcasted_iota(jnp.int32, (owners * rows, 2 * held), 1)
    route_ref[...] = jnp.where(place == wanted, 1.0, 0.0).T.astype(jnp.bfloat16)

    for step in range(1, n_dp):
        grad_copy(step).wait_send()
        grad_arrival(step).wait_recv()
    own_grad.wait()
    own_slots.wait()
    lax.fori_loop(0, owners, finish, 0)


def update(
    n_dp,
    offset_ref,
    route_ref,
    arrived_ref,
    grads_ref,
    master_ref,
    m_codes_ref,
    m_scale_ref,
    v_codes_ref,
    v_scale_ref,
    adam_ref,
    weight_ref,
    m_all,
    v_all,
    peaks,
):
    step = pl.program_id(0)
    held, width = master_ref.shape
    offset = offset_ref[0]
    placed = jnp.dot(route_ref[...], arrived_ref[...], preferred_element_type=jnp.float32)
    grad = grads_ref[0].astype(jnp.float32)
    for replica in range(1, n_dp):
        grad = grad + grads_ref[replica].astype(jnp.float32)
    m_next = FIRST_DECAY * placed[:held] + (1.0 - FIRST_DECAY) * grad
    v_next = SECOND_DECAY * placed[held:] + (1.0 - SECOND_DECAY) * grad * grad
    master = master_ref[...]
    adam = (m_next * (1.0 / FIRST_CORRECTION)) / (
        jnp.sqrt(v_next * (1.0 / SECOND_CORRECTION)) + ADAM_EPSILON
    ) + WEIGHT_DECAY * master
    adam_ref[...] = adam
    weight_ref[...] = (master - LEARN_RATE * adam).astype(jnp.bfloat16)
    m_all[step] = m_next
    v_all[step] = v_next
    column = lax.broadcasted_iota(jnp.int32, (held, width), 1)
    head = column < offset - step * width

    @pl.when(step == 0)
    def _():
        peaks[...] = jnp.zeros_like(peaks)

    for at, values in ((0, m_next), (2, v_next)):
        size = jnp.abs(values)
        fore = jnp.where(head, size, 0.0)
        rear = jnp.where(head, 0.0, size)
        for part, half in ((0, fore), (1, rear)):
            best = peaks[at + part]
            for lane in range(0, width, 128):
                best = jnp.maximum(best, half[:, lane : lane + 128])
            peaks[at + part] = best

    @pl.when(step == pl.num_programs(0) - 1)
    def _():
        line = lax.broadcasted_iota(jnp.int32, (held, held), 0)
        for at, values, codes_ref, scale_ref in (
            (0, m_all, m_codes_ref, m_scale_ref),
            (2, v_all, v_codes_ref, v_scale_ref),
        ):
            fore = jnp.broadcast_to(jnp.max(peaks[at], axis=1, keepdims=True), (held, held))
            rear = jnp.broadcast_to(jnp.max(peaks[at + 1], axis=1, keepdims=True), (held, held))
            above = jnp.where(line == 0, 0.0, pltpu.roll(rear, 1, 0))
            below = jnp.where(line == held - 1, 0.0, pltpu.roll(fore, held - 1, 0))
            first = jnp.maximum(above, fore) + 1e-06
            second = jnp.maximum(rear, below) + 1e-06
            scale_ref[:, :held] = first.T[:1, :]
            scale_ref[:, held : held + 1] = second[held - 1 :, :1]
            first = (1.0 / first)[:, :1]
            second = (1.0 / second)[:, :1]
            for part in range(values.shape[0]):
                left = column < offset - part * width
                codes_ref[:, part * width : (part + 1) * width] = (
                    values[part] * jnp.where(left, first, second)
                ).astype(jnp.bfloat16)


def local(
    n_dp,
    n_tensor,
    old_m_codes,
    old_m_scale,
    old_v_codes,
    old_v_scale,
    block_target,
    new_offset,
    grad_part,
    master_weight,
):
    owners = n_dp * n_tensor
    held, size = old_m_codes.shape
    capacity = max(2, 2 * held // owners)
    rows = -(-2 * capacity // 16) * 16
    vmem = pl.BlockSpec(memory_space=pltpu.VMEM)
    hbm = pl.BlockSpec(memory_space=pl.ANY)
    arrived, grads, route = pl.pallas_call(
        functools.partial(exchange, n_dp, n_tensor, capacity),
        out_shape=(
            jax.ShapeDtypeStruct((owners, rows, size), jnp.bfloat16),
            jax.ShapeDtypeStruct((n_dp, held, size), jnp.bfloat16),
            jax.ShapeDtypeStruct((2 * held, owners * rows), jnp.bfloat16),
        ),
        in_specs=[vmem] * 5 + [hbm],
        out_specs=(hbm, hbm, vmem),
        scratch_shapes=[
            pltpu.VMEM((owners, rows, size), jnp.bfloat16),
            pltpu.SemaphoreType.DMA((owners,)),
            pltpu.SemaphoreType.DMA((owners,)),
            pltpu.SemaphoreType.DMA((n_dp,)),
            pltpu.SemaphoreType.DMA((n_dp,)),
            pltpu.SemaphoreType.DMA((2,)),
        ],
        compiler_params=pltpu.CompilerParams(
            collective_id=0, has_side_effects=True, vmem_limit_bytes=48 * 1024 * 1024
        ),
    )(
        block_target.reshape(owners, held),
        old_m_codes,
        old_m_scale.reshape(1, held),
        old_v_codes,
        old_v_scale.reshape(1, held),
        grad_part[0, 0],
    )
    width = 512
    whole = lambda shape: pl.BlockSpec(shape, lambda i: (0, 0))
    part = pl.BlockSpec((held, width), lambda i: (0, i))
    m_codes, m_scale, v_codes, v_scale, adam, weight = pl.pallas_call(
        functools.partial(update, n_dp),
        grid=(size // width,),
        out_shape=(
            jax.ShapeDtypeStruct((held, size), jnp.bfloat16),
            jax.ShapeDtypeStruct((1, held + 1), jnp.float32),
            jax.ShapeDtypeStruct((held, size), jnp.bfloat16),
            jax.ShapeDtypeStruct((1, held + 1), jnp.float32),
            jax.ShapeDtypeStruct((held, size), jnp.float32),
            jax.ShapeDtypeStruct((held, size), jnp.bfloat16),
        ),
        in_specs=[
            pl.BlockSpec(memory_space=pltpu.SMEM),
            whole((2 * held, owners * rows)),
            pl.BlockSpec((owners * rows, width), lambda i: (0, i)),
            pl.BlockSpec((n_dp, held, width), lambda i: (0, 0, i)),
            part,
        ],
        out_specs=(
            whole((held, size)),
            whole((1, held + 1)),
            whole((held, size)),
            whole((1, held + 1)),
            part,
            part,
        ),
        scratch_shapes=[
            pltpu.VMEM((size // width, held, width), jnp.float32),
            pltpu.VMEM((size // width, held, width), jnp.float32),
            pltpu.VMEM((4, held, 128), jnp.float32),
        ],
        compiler_params=pltpu.CompilerParams(
            dimension_semantics=("arbitrary",), vmem_limit_bytes=48 * 1024 * 1024
        ),
    )(
        new_offset,
        route,
        arrived.reshape(owners * rows, size),
        grads,
        master_weight[0],
    )
    return (
        m_codes.reshape(1, held, size),
        m_scale,
        v_codes.reshape(1, held, size),
        v_scale,
        adam.reshape(1, held, size),
        weight.reshape(1, held, size),
    )


def solution(mesh):
    return jax.shard_map(
        functools.partial(local, mesh.shape["dp"], mesh.shape["tensor"]),
        mesh=mesh,
        in_specs=(
            P(("dp", "tensor"), None),
            P(("dp", "tensor")),
            P(("dp", "tensor"), None),
            P(("dp", "tensor")),
            P(),
            P(("dp", "tensor")),
            P("dp", "tensor", None, None),
            P("tensor", "dp", None),
        ),
        out_specs=(
            P("tensor", "dp", None),
            P(("dp", "tensor"), None),
            P("tensor", "dp", None),
            P(("dp", "tensor"), None),
            P("tensor", "dp", None),
            P("tensor", "dp", None),
        ),
        check_vma=False,
    )
```

time: 192 us -> 66.7 us (0.35)
  waiting for transfers between devices: 94.3 us -> 0 us
  Pallas kernels: 0 us -> 60.1 us
  local copies, waits for them, and re-layouts: 61 us -> 4.11 us
  between operations: 14.9 us -> 1.41 us
  other arithmetic: 13.3 us -> 0 us
  starting transfers between devices: 7.71 us -> 0 us
    all_to_all x1 -> x0, waiting for transfers between devices: 93.8 us -> none  [local(): lax.all_to_all(outgoing.reshape(owners, capacity, 2, size), ('dp', 'tenso...]
    pallas_call x0 -> x2, Pallas kernels: none -> 60.1 us  [the longest x1 55.5 us: local(): pl.pallas_call(functools.partial(exchange, n_dp, n_tensor, capacity), out...]
    scatter x2 -> x0, local copies, waits for them, and re-layouts: 31.2 us -> none  [the longest x1 15.7 us: local(): jnp.zeros((owners * capacity, 2, size), jnp.float32).at[place].set(moments)]
    dynamic_update_slice x2 -> x0, local copies, waits for them, and re-layouts: 14 us -> none  [requantize(): lax.dynamic_update_slice(jnp.zeros(((held + 1) * size,), jnp.float32), fl...]
    all_to_all x1 -> x0, starting transfers between devices: 7.49 us -> none  [local(): lax.all_to_all(outgoing.reshape(owners, capacity, 2, size), ('dp', 'tenso...]
    gather x2 -> x0, local copies, waits for them, and re-layouts: 5.62 us -> none  [the longest x1 4.97 us: local(): placed = arrived.reshape(owners * capacity, 2, size)[pick]]
    reshape x1 -> x0, other arithmetic: 4.48 us -> none  [local(): new_weight.reshape(1, held, size)]
    broadcast_in_dim x1 -> x0, local copies, waits for them, and re-layouts: 4.1 us -> none  [local(): jnp.zeros((owners * capacity, 2, size), jnp.float32).at[place].set(moments)]
  transfers between devices with their start and end apart: 2 -> 0, of which waited for: 1 -> 0; matrix products, arithmetic and copies ran while one was open for 4% -> 0% of each run, Pallas kernels for 0% -> 0%
where the time goes in v1:
time: 66.7 us; the launch traced here: 65.6 us
  Pallas kernels  60.1 us (90%)
  local copies, waits for them, and re-layouts  4.11 us (6%)
  between operations  1.41 us (2%)
    pallas_call x1, Pallas kernels, local(): pl.pallas_call(functools.partial(exchange, n_dp, n_tensor, capacity), out...  55.5 us
    pallas_call x1, Pallas kernels, local(): pl.pallas_call(functools.partial(update, n_dp), grid=(size // width,), ou...  4.6 us
    unnamed x12, local copies, waits for them, and re-layouts  4.11 us

profile of v1, /device:TPU:0, one launch (start us, length us, event | category | flops | bytes accessed | tf_op | source)
XLA Modules:
  0.0 65.6 jit_solution(4526831609921756074)
XLA Ops:
  0.6 0.0 copy-start
  1.4 0.0 copy-start.1
  1.4 1.0 %copy-done.1 = bf16[128,2048]{1,0:T(8,128)(2,1)S(1)} copy-done((bf16[128,2048]{1,0:T(8,128)(2,1)S(1)}, bf16[128,2048]{1,0:T(8,128)(2,1)}, u32[]{:S(2)}) %copy-start.1) | copy-done | bytes 524312
  2.4 0.0 copy-start.2
  2.4 1.0 %copy-done.2 = bf16[128,2048]{1,0:T(8,128)(2,1)S(1)} copy-done((bf16[128,2048]{1,0:T(8,128)(2,1)S(1)}, bf16[128,2048]{1,0:T(8,128)(2,1)}, u32[]{:S(2)}) %copy-start.2) | copy-done | bytes 524312
  3.5 0.0 copy-start.3
  3.5 0.7 %copy-done.3 = s32[4096]{0:T(1024)S(1)} copy-done((s32[4096]{0:T(1024)S(1)}, s32[4096]{0:T(1024)}, u32[]{:S(2)}) %copy-start.3) | copy-done | bytes 16408
  4.2 0.0 copy-start.4
  4.2 0.7 copy-done.4
  4.8 0.0 copy-start.5
  4.8 0.7 copy-done.5
  5.5 55.5 %shard_map.127 = (bf16[32,16,2048]{2,1,0:T(8,128)(2,1)S(1)}, bf16[4,128,2048]{2,1,0:T(8,128)(2,1)S(1)}, bf16[256,512]{1,0:T(8,128)(2,1)S(1)}) custom-call(s32[32,128]{1,0:T(8,128)S(1)} %bitcast.12, bf16[128,2048]{1,0:T(8,128)(2,1)S(1)} %copy-done.1, f32[1,128]{1,0:T(1,128)S(1)} %bitcast.13, bf16[128,2048]{1,0:T(8,128)(2,1)S(1)} %copy-done.2, ...), custom_call_target="tpu_custom_call" | custom-call | tf_op jit(solution)/shard_map/pallas_call | solution.py:279
  61.0 0.0 copy-done
  61.0 4.6 %shard_map.128 = (bf16[128,2048]{1,0:T(8,128)(2,1)}, f32[1,129]{1,0:T(1,128)}, bf16[128,2048]{1,0:T(8,128)(2,1)}, f32[1,129]{1,0:T(1,128)}, f32[128,2048]{1,0:T(8,128)}, /*index=5*/bf16[128,2048]{1,0:T(8,128)(2,1)}) custom-call(s32[1]{0:T(128)S(6)} %copy.14.offset_ref, bf16[256,512]{1,0:T(8,128)(2,1)S(1)} %get-tuple-element.15.route_ref, ...), custom_call_target="tpu_custom_call" | custom-call | tf_op jit(solution)/shard_map/pallas_call | solution.py:310
Async XLA Ops:
  0.6 60.4 %copy-start = (f32[1,128,2048]{2,1,0:T(8,128)S(1)}, f32[1,128,2048]{2,1,0:T(8,128)}, u32[]{:S(2)}) copy-start(f32[1,128,2048]{2,1,0:T(8,128)} %param.15) | copy-start | bytes 3145732
  1.4 1.0 %copy-start.1 = (bf16[128,2048]{1,0:T(8,128)(2,1)S(1)}, bf16[128,2048]{1,0:T(8,128)(2,1)}, u32[]{:S(2)}) copy-start(bf16[128,2048]{1,0:T(8,128)(2,1)} %m_codes_ref.1) | copy-start | bytes 1572868
  2.4 1.0 %copy-start.2 = (bf16[128,2048]{1,0:T(8,128)(2,1)S(1)}, bf16[128,2048]{1,0:T(8,128)(2,1)}, u32[]{:S(2)}) copy-start(bf16[128,2048]{1,0:T(8,128)(2,1)} %v_codes_ref.1) | copy-start | bytes 1572868
  3.5 0.7 %copy-start.3 = (s32[4096]{0:T(1024)S(1)}, s32[4096]{0:T(1024)}, u32[]{:S(2)}) copy-start(s32[4096]{0:T(1024)} %param.12) | copy-start | bytes 49156
  4.2 0.7 copy-start.4
  4.8 0.7 copy-start.5

commit v2 on v1

--- a/solution.py
+++ b/solution.py
@@ -25,28 +25,45 @@
     n_dp,
     n_tensor,
     capacity,
+    targets_hbm,
+    m_codes_hbm,
+    m_scale_hbm,
+    v_codes_hbm,
+    v_scale_hbm,
+    grad_ref,
+    arrived_ref,
+    total_ref,
+    route_ref,
     targets_ref,
     m_codes_ref,
     m_scale_ref,
     v_codes_ref,
     v_scale_ref,
-    grad_ref,
-    arrived_ref,
-    grads_ref,
-    route_ref,
     outgoing,
+    grad_own,
+    grad_pair,
+    grad_out,
+    grad_in,
+    total,
+    route,
     send_sem,
     recv_sem,
+    pair_send_sem,
+    pair_recv_sem,
     grad_send_sem,
     grad_recv_sem,
+    own_sem,
     local_sem,
 ):
     owners = n_dp * n_tensor
     held, size = m_codes_ref.shape
     rows = outgoing.shape[1]
+    n_x = n_dp // 2
     my_dp = lax.axis_index("dp")
     my_tensor = lax.axis_index("tensor")
     myself = my_dp * n_tensor + my_tensor
+    my_x = my_dp // 2
+    my_core = lax.rem(my_dp, 2)
 
     barrier = pltpu.get_barrier_semaphore()
 
@@ -57,8 +74,32 @@
         )
         return carry
 
+    loads = [
+        pltpu.make_async_copy(source, target, local_sem.at[i])
+        for i, (source, target) in enumerate(
+            (
+                (targets_hbm, targets_ref),
+                (m_scale_hbm, m_scale_ref),
+                (v_scale_hbm, v_scale_ref),
+                (m_codes_hbm, m_codes_ref),
+                (v_codes_hbm, v_codes_ref),
+            )
+        )
+    ]
+    for load in loads:
+        load.start()
     lax.fori_loop(1, owners, greet, 0)
 
+    def share(x, core):
+        return grad_ref.at[pl.ds(pl.multiple_of((2 * x + core) * held, held), held)]
+
+    own_loads = [
+        pltpu.make_async_copy(share(x, my_core), grad_own.at[x], own_sem.at[x]) for x in range(n_x)
+    ]
+    for load in own_loads:
+        load.start()
+
+    loads[0].wait()
     mine = targets_ref[pl.ds(myself, 1), :]
     owner = (mine // held).astype(jnp.float32)
     owner_col = column_of(owner, held)
@@ -70,90 +111,91 @@
     )
     slot = (owner * rows + rank).astype(jnp.int32)
     slots = jnp.concatenate([slot, slot + capacity], axis=1)
+    for load in loads[1:]:
+        load.wait()
     m_old = m_codes_ref[...].astype(jnp.float32) * column_of(m_scale_ref[...], held)[:, :1]
     v_old = v_codes_ref[...].astype(jnp.float32) * column_of(v_scale_ref[...], held)[:, :1]
     moments = jnp.concatenate([m_old.astype(jnp.bfloat16), v_old.astype(jnp.bfloat16)], axis=0)
-    some = 8
-    for first in range(0, owners, some):
-        place = lax.broadcasted_iota(jnp.int32, (some * rows, 2 * held), 0) + first * rows
+
+    pair_copies = [
+        pltpu.make_async_remote_copy(
+            src_ref=share(x, 1 - my_core),
+            dst_ref=grad_pair.at[x],
+            send_sem=pair_send_sem.at[x],
+            recv_sem=pair_recv_sem.at[x],
+            device_id=(2 * my_x + 1 - my_core, my_tensor),
+            device_id_type=MESH,
+        )
+        for x in range(n_x)
+    ]
+
+    def grad_copy(step):
+        other = lax.rem(my_x + step, n_x)
+        return pltpu.make_async_remote_copy(
+            src_ref=grad_out.at[other],
+            dst_ref=grad_in.at[my_x],
+            send_sem=grad_send_sem.at[other],
+            recv_sem=grad_recv_sem.at[my_x],
+            device_id=(2 * other + my_core, my_tensor),
+            device_id_type=MESH,
+        )
+
+    def grad_arrival(step):
+        other = lax.rem(my_x + step, n_x)
+        return pltpu.make_async_remote_copy(
+            src_ref=grad_out.at[other],
+            dst_ref=grad_in.at[other],
+            send_sem=grad_send_sem.at[other],
+            recv_sem=grad_recv_sem.at[other],
+            device_id=(2 * other + my_core, my_tensor),
+            device_id_type=MESH,
+        )
+
+    def copy_to(there, lane, other, landing, arrival):
+        return pltpu.make_async_remote_copy(
+            src_ref=outgoing.at[other],
+            dst_ref=arrived_ref.at[landing],
+            send_sem=send_sem.at[other],
+            recv_sem=recv_sem.at[arrival],
+            device_id=(there, lane),
+            device_id_type=MESH,
+        )
+
+    for group in range(n_dp):
+        there = lax.rem(my_dp + group + 1, n_dp)
+        base = there * n_tensor
+        place = lax.broadcasted_iota(jnp.int32, (n_tensor * rows, 2 * held), 0) + base * rows
         chosen = jnp.where(place == slots, 1.0, 0.0).astype(jnp.bfloat16)
         packed = jnp.dot(chosen, moments, preferred_element_type=jnp.float32)
-        outgoing[first : first + some] = packed.astype(jnp.bfloat16).reshape(some, rows, size)
-
-    pl.semaphore_wait(barrier, owners - 1)
-
-    def grad_copy(step):
-        other = lax.rem(my_dp + step, n_dp)
-        return pltpu.make_async_remote_copy(
-            src_ref=grad_ref.at[pl.ds(pl.multiple_of(other * held, held), held)],
-            dst_ref=grads_ref.at[my_dp],
-            send_sem=grad_send_sem.at[other],
-            recv_sem=grad_recv_sem.at[my_dp],
-            device_id=(other, my_tensor),
-            device_id_type=MESH,
-        )
-
-    def grad_arrival(step):
-        other = lax.rem(my_dp + step, n_dp)
-        return pltpu.make_async_remote_copy(
-            src_ref=grad_ref.at[pl.ds(pl.multiple_of(other * held, held), held)],
-            dst_ref=grads_ref.at[other],
-            send_sem=grad_send_sem.at[other],
-            recv_sem=grad_recv_sem.at[other],
-            device_id=(other, my_tensor),
-            device_id_type=MESH,
-        )
-
-    def peer(step):
-        tensor_step = lax.rem(step // n_dp + n_tensor // 2, n_tensor)
-        dp_step = lax.rem(step, n_dp)
-        there = lax.rem(my_dp + dp_step, n_dp)
-        across = lax.rem(my_tensor + tensor_step, n_tensor)
-        return there, across, there * n_tensor + across, (tensor_step + dp_step) > 0
-
-    def send(step, carry):
-        there, across, other, remote = peer(step)
-
-        @pl.when(remote)
-        def _():
-            pltpu.make_async_remote_copy(
-                src_ref=outgoing.at[other],
-                dst_ref=arrived_ref.at[myself],
-                send_sem=send_sem.at[other],
-                recv_sem=recv_sem.at[myself],
-                device_id=(there, across),
-                device_id_type=MESH,
-            ).start()
-
-        return carry
-
-    def finish(step, carry):
-        there, across, other, remote = peer(step)
-
-        @pl.when(remote)
-        def _():
-            copy = pltpu.make_async_remote_copy(
-                src_ref=outgoing.at[other],
-                dst_ref=arrived_ref.at[other],
-                send_sem=send_sem.at[other],
-                recv_sem=recv_sem.at[other],
-                device_id=(there, across),
-                device_id_type=MESH,
-            )
-            copy.wait_send()
-            copy.wait_recv()
-
-        return carry
-
-    lax.fori_loop(0, owners, send, 0)
-    for step in range(1, n_dp):
+        outgoing[pl.ds(base, n_tensor)] = packed.astype(jnp.bfloat16).reshape(n_tensor, rows, size)
+        if group == 0:
+            pl.semaphore_wait(barrier, owners - 1)
+            for copy in pair_copies:
+                copy.start()
+        last = group == n_dp - 1
+
+        def send(step, carry, there=there, base=base):
+            lane = lax.rem(my_tensor + step, n_tensor)
+            copy_to(there, lane, base + lane, myself, myself).start()
+            return carry
+
+        half = n_tensor // 2
+        lax.fori_loop(half, n_tensor, send, 0)
+        lax.fori_loop(1 if last else 0, half, send, 0)
+    own_slots = pltpu.make_async_copy(outgoing.at[myself], arrived_ref.at[myself], local_sem.at[5])
+    own_slots.start()
+
+    for load in own_loads:
+        load.wait()
+    for copy in pair_copies:
+        copy.wait_send()
+        copy.wait_recv()
+    for step in range(1, n_x):
+        other = lax.rem(my_x + step, n_x)
+        grad_out[other] = (
+            grad_own[other].astype(jnp.float32) + grad_pair[other].astype(jnp.float32)
+        ).astype(jnp.bfloat16)
         grad_copy(step).start()
-    own_grad = pltpu.make_async_copy(
-        grad_ref.at[pl.ds(pl.multiple_of(my_dp * held, held), held)], grads_ref.at[my_dp], local_sem.at[0]
-    )
-    own_grad.start()
-    own_slots = pltpu.make_async_copy(outgoing.at[myself], arrived_ref.at[myself], local_sem.at[1])
-    own_slots.start()
 
     targets = targets_ref[...]
     is_mine = jnp.where(targets // held == myself, 1.0, 0.0)
@@ -173,22 +215,37 @@
     place = jnp.where((place >= 0) & (index >= capacity), place + held, place)
     place = jnp.where(index < 2 * capacity, place, -1)
     wanted = lax.broadcasted_iota(jnp.int32, (owners * rows, 2 * held), 1)
-    route_ref[...] = jnp.where(place == wanted, 1.0, 0.0).T.astype(jnp.bfloat16)
-
-    for step in range(1, n_dp):
+    route[...] = jnp.where(place == wanted, 1.0, 0.0).T.astype(jnp.bfloat16)
+    route_out = pltpu.make_async_copy(route, route_ref, local_sem.at[6])
+    route_out.start()
+
+    grad = grad_own[my_x].astype(jnp.float32) + grad_pair[my_x].astype(jnp.float32)
+    for step in range(1, n_x):
         grad_copy(step).wait_send()
         grad_arrival(step).wait_recv()
-    own_grad.wait()
+        grad = grad + grad_in[lax.rem(my_x + step, n_x)].astype(jnp.float32)
+    total[...] = grad
+    total_out = pltpu.make_async_copy(total, total_ref, local_sem.at[7])
+    total_out.start()
+
+    def finish(step, carry):
+        other = lax.rem(myself + step, owners)
+        copy = copy_to(other // n_tensor, lax.rem(other, n_tensor), other, other, other)
+        copy.wait_send()
+        copy.wait_recv()
+        return carry
+
     own_slots.wait()
-    lax.fori_loop(0, owners, finish, 0)
+    lax.fori_loop(1, owners, finish, 0)
+    route_out.wait()
+    total_out.wait()
 
 
 def update(
-    n_dp,
     offset_ref,
     route_ref,
     arrived_ref,
-    grads_ref,
+    grad_ref,
     master_ref,
     m_codes_ref,
     m_scale_ref,
@@ -204,9 +261,7 @@
     held, width = master_ref.shape
     offset = offset_ref[0]
     placed = jnp.dot(route_ref[...], arrived_ref[...], preferred_element_type=jnp.float32)
-    grad = grads_ref[0].astype(jnp.float32)
-    for replica in range(1, n_dp):
-        grad = grad + grads_ref[replica].astype(jnp.float32)
+    grad = grad_ref[...]
     m_next = FIRST_DECAY * placed[:held] + (1.0 - FIRST_DECAY) * grad
     v_next = SECOND_DECAY * placed[held:] + (1.0 - SECOND_DECAY) * grad * grad
     master = master_ref[...]
@@ -274,27 +329,41 @@
     held, size = old_m_codes.shape
     capacity = max(2, 2 * held // owners)
     rows = -(-2 * capacity // 16) * 16
-    vmem = pl.BlockSpec(memory_space=pltpu.VMEM)
     hbm = pl.BlockSpec(memory_space=pl.ANY)
-    arrived, grads, route = pl.pallas_call(
+    n_x = n_dp // 2
+    arrived, grad, route = pl.pallas_call(
         functools.partial(exchange, n_dp, n_tensor, capacity),
         out_shape=(
             jax.ShapeDtypeStruct((owners, rows, size), jnp.bfloat16),
-            jax.ShapeDtypeStruct((n_dp, held, size), jnp.bfloat16),
+            jax.ShapeDtypeStruct((held, size), jnp.float32),
             jax.ShapeDtypeStruct((2 * held, owners * rows), jnp.bfloat16),
         ),
-        in_specs=[vmem] * 5 + [hbm],
-        out_specs=(hbm, hbm, vmem),
+        in_specs=[hbm] * 6,
+        out_specs=(hbm, hbm, hbm),
         scratch_shapes=[
+            pltpu.VMEM((owners, held), jnp.int32),
+            pltpu.VMEM((held, size), jnp.bfloat16),
+            pltpu.VMEM((1, held), jnp.float32),
+            pltpu.VMEM((held, size), jnp.bfloat16),
+            pltpu.VMEM((1, held), jnp.float32),
             pltpu.VMEM((owners, rows, size), jnp.bfloat16),
+            pltpu.VMEM((n_x, held, size), jnp.bfloat16),
+            pltpu.VMEM((n_x, held, size), jnp.bfloat16),
+            pltpu.VMEM((n_x, held, size), jnp.bfloat16),
+            pltpu.VMEM((n_x, held, size), jnp.bfloat16),
+            pltpu.VMEM((held, size), jnp.float32),
+            pltpu.VMEM((2 * held, owners * rows), jnp.bfloat16),
             pltpu.SemaphoreType.DMA((owners,)),
             pltpu.SemaphoreType.DMA((owners,)),
-            pltpu.SemaphoreType.DMA((n_dp,)),
-            pltpu.SemaphoreType.DMA((n_dp,)),
-            pltpu.SemaphoreType.DMA((2,)),
+            pltpu.SemaphoreType.DMA((n_x,)),
+            pltpu.SemaphoreType.DMA((n_x,)),
+            pltpu.SemaphoreType.DMA((n_x,)),
+            pltpu.SemaphoreType.DMA((n_x,)),
+            pltpu.SemaphoreType.DMA((n_x,)),
+            pltpu.SemaphoreType.DMA((8,)),
         ],
         compiler_params=pltpu.CompilerParams(
-            collective_id=0, has_side_effects=True, vmem_limit_bytes=48 * 1024 * 1024
+            collective_id=0, has_side_effects=True, vmem_limit_bytes=60 * 1024 * 1024
         ),
     )(
         block_target.reshape(owners, held),
@@ -308,7 +377,7 @@
     whole = lambda shape: pl.BlockSpec(shape, lambda i: (0, 0))
     part = pl.BlockSpec((held, width), lambda i: (0, i))
     m_codes, m_scale, v_codes, v_scale, adam, weight = pl.pallas_call(
-        functools.partial(update, n_dp),
+        update,
         grid=(size // width,),
         out_shape=(
             jax.ShapeDtypeStruct((held, size), jnp.bfloat16),
@@ -322,7 +391,7 @@
             pl.BlockSpec(memory_space=pltpu.SMEM),
             whole((2 * held, owners * rows)),
             pl.BlockSpec((owners * rows, width), lambda i: (0, i)),
-            pl.BlockSpec((n_dp, held, width), lambda i: (0, 0, i)),
+            part,
             part,
         ],
         out_specs=(
@@ -339,13 +408,13 @@
             pltpu.VMEM((4, held, 128), jnp.float32),
         ],
         compiler_params=pltpu.CompilerParams(
-            dimension_semantics=("arbitrary",), vmem_limit_bytes=48 * 1024 * 1024
+            dimension_semantics=("arbitrary",), vmem_limit_bytes=60 * 1024 * 1024
         ),
     )(
         new_offset,
         route,
         arrived.reshape(owners * rows, size),
-        grads,
+        grad,
         master_weight[0],
     )
     return (

time: 66.7 us -> 62.9 us (0.943); the launches traced: 65.6 us -> 62.7 us
  local copies, waits for them, and re-layouts: 4.11 us -> 0 us
  Pallas kernels: 60.1 us -> 61.4 us
    unnamed x12 -> x0, local copies, waits for them, and re-layouts: 4.11 us -> none
    pallas_call x1, Pallas kernels: 4.6 us -> 6.33 us  [local(): pl.pallas_call(update, grid=(size // width,), out_shape=(jax.ShapeDtypeSt...]
where the time goes in v2:
time: 62.9 us; the launch traced here: 62.7 us
  Pallas kernels  61.4 us (98%)
  between operations  1.29 us (2%)
    pallas_call x1, Pallas kernels, local(): pl.pallas_call(functools.partial(exchange, n_dp, n_tensor, capacity), out...  55 us
    pallas_call x1, Pallas kernels, local(): pl.pallas_call(update, grid=(size // width,), out_shape=(jax.ShapeDtypeSt...  6.33 us

profile of v2, /device:TPU:0, one launch (start us, length us, event | category | flops | bytes accessed | tf_op | source)
XLA Modules:
  0.0 62.7 jit_solution(2461098636757605057)
XLA Ops:
  1.3 55.0 %shard_map.127 = (bf16[32,16,2048]{2,1,0:T(8,128)(2,1)}, f32[128,2048]{1,0:T(8,128)}, bf16[256,512]{1,0:T(8,128)(2,1)}) custom-call(s32[32,128]{1,0:T(8,128)} %bitcast.13, bf16[128,2048]{1,0:T(8,128)(2,1)} %m_codes_hbm.1, f32[1,128]{1,0:T(1,128)} %bitcast.14, bf16[128,2048]{1,0:T(8,128)(2,1)} %v_codes_hbm.1, f32[1,128]{1,0:T(1,128)} %bitcast.15, ...), custom_call_target="tpu_custom_call" | custom-call | tf_op jit(solution)/shard_map/pallas_call | solution.py:334
  56.3 6.3 %shard_map.128 = (bf16[128,2048]{1,0:T(8,128)(2,1)}, f32[1,129]{1,0:T(1,128)}, bf16[128,2048]{1,0:T(8,128)(2,1)}, f32[1,129]{1,0:T(1,128)}, f32[128,2048]{1,0:T(8,128)}, /*index=5*/bf16[128,2048]{1,0:T(8,128)(2,1)}) custom-call(s32[1]{0:T(128)S(6)} %copy.14.offset_ref, bf16[256,512]{1,0:T(8,128)(2,1)} %get-tuple-element.15.route_ref, ...), custom_call_target="tpu_custom_call" | custom-call | tf_op jit(solution)/shard_map/pallas_call | solution.py:379

commit v3 on v2

--- a/solution.py
+++ b/solution.py
@@ -180,8 +180,18 @@
             return carry
 
         half = n_tensor // 2
-        lax.fori_loop(half, n_tensor, send, 0)
-        lax.fori_loop(1 if last else 0, half, send, 0)
+        if group < n_dp - 1:
+            lax.fori_loop(0, half, send, 0)
+        else:
+            lax.fori_loop(1, half, send, 0)
+
+            def far(step, carry):
+                for back in range(n_dp):
+                    there2 = lax.rem(my_dp + back + 1, n_dp)
+                    send(step, 0, there=there2, base=there2 * n_tensor)
+                return carry
+
+            lax.fori_loop(half, n_tensor, far, 0)
     own_slots = pltpu.make_async_copy(outgoing.at[myself], arrived_ref.at[myself], local_sem.at[5])
     own_slots.start()
 
@@ -373,7 +383,7 @@
         old_v_scale.reshape(1, held),
         grad_part[0, 0],
     )
-    width = 512
+    width = 1024
     whole = lambda shape: pl.BlockSpec(shape, lambda i: (0, 0))
     part = pl.BlockSpec((held, width), lambda i: (0, i))
     m_codes, m_scale, v_codes, v_scale, adam, weight = pl.pallas_call(

time: 62.9 us -> 60 us (0.954)
  the two profiles are of different devices: /device:TPU:0 before, /device:TPU:13 now
where the time goes in v3:
time: 60 us; the launch traced here: 59.8 us
  Pallas kernels  58.5 us (98%)
  between operations  1.29 us (2%)
    pallas_call x1, Pallas kernels, local(): pl.pallas_call(functools.partial(exchange, n_dp, n_tensor, capacity), out...  52.9 us
    pallas_call x1, Pallas kernels, local(): pl.pallas_call(update, grid=(size // width,), out_shape=(jax.ShapeDtypeSt...  5.59 us

profile of v3, /device:TPU:13, one launch (start us, length us, event | category | flops | bytes accessed | tf_op | source)
XLA Modules:
  0.0 59.8 jit_solution(6379641191889570318)
XLA Ops:
  1.3 52.9 %shard_map.127 = (bf16[32,16,2048]{2,1,0:T(8,128)(2,1)}, f32[128,2048]{1,0:T(8,128)}, bf16[256,512]{1,0:T(8,128)(2,1)}) custom-call(s32[32,128]{1,0:T(8,128)} %bitcast.13, bf16[128,2048]{1,0:T(8,128)(2,1)} %m_codes_hbm.1, f32[1,128]{1,0:T(1,128)} %bitcast.14, bf16[128,2048]{1,0:T(8,128)(2,1)} %v_codes_hbm.1, f32[1,128]{1,0:T(1,128)} %bitcast.15, ...), custom_call_target="tpu_custom_call" | custom-call | tf_op jit(solution)/shard_map/pallas_call | solution.py:344
  54.2 5.6 %shard_map.128 = (bf16[128,2048]{1,0:T(8,128)(2,1)}, f32[1,129]{1,0:T(1,128)}, bf16[128,2048]{1,0:T(8,128)(2,1)}, f32[1,129]{1,0:T(1,128)}, f32[128,2048]{1,0:T(8,128)}, /*index=5*/bf16[128,2048]{1,0:T(8,128)(2,1)}) custom-call(s32[1]{0:T(128)S(6)} %copy.14.offset_ref, bf16[256,512]{1,0:T(8,128)(2,1)} %get-tuple-element.15.route_ref, ...), custom_call_target="tpu_custom_call" | custom-call | tf_op jit(solution)/shard_map/pallas_call | solution.py:389

commit v4 on v3

--- a/solution.py
+++ b/solution.py
@@ -383,7 +383,7 @@
         old_v_scale.reshape(1, held),
         grad_part[0, 0],
     )
-    width = 1024
+    width = 2048
     whole = lambda shape: pl.BlockSpec(shape, lambda i: (0, 0))
     part = pl.BlockSpec((held, width), lambda i: (0, i))
     m_codes, m_scale, v_codes, v_scale, adam, weight = pl.pallas_call(

time: 60 us -> 59.9 us (level)
  no operation moved by 1% of the time
where the time goes in v4:
time: 59.9 us; the launch traced here: 59.7 us
  Pallas kernels  58.4 us (97%)
  between operations  1.29 us (2%)
    pallas_call x1, Pallas kernels, local(): pl.pallas_call(functools.partial(exchange, n_dp, n_tensor, capacity), out...  52.9 us
    pallas_call x1, Pallas kernels, local(): pl.pallas_call(update, grid=(size // width,), out_shape=(jax.ShapeDtypeSt...  5.51 us

profile of v4, /device:TPU:13, one launch (start us, length us, event | category | flops | bytes accessed | tf_op | source)
XLA Modules:
  0.0 59.7 jit_solution(7995974005231070992)
XLA Ops:
  1.3 52.9 %shard_map.127 = (bf16[32,16,2048]{2,1,0:T(8,128)(2,1)}, f32[128,2048]{1,0:T(8,128)}, bf16[256,512]{1,0:T(8,128)(2,1)}) custom-call(s32[32,128]{1,0:T(8,128)} %bitcast.13, bf16[128,2048]{1,0:T(8,128)(2,1)} %m_codes_hbm.1, f32[1,128]{1,0:T(1,128)} %bitcast.14, bf16[128,2048]{1,0:T(8,128)(2,1)} %v_codes_hbm.1, f32[1,128]{1,0:T(1,128)} %bitcast.15, ...), custom_call_target="tpu_custom_call" | custom-call | tf_op jit(solution)/shard_map/pallas_call | solution.py:344
  54.2 5.5 %shard_map.128 = (bf16[128,2048]{1,0:T(8,128)(2,1)}, f32[1,129]{1,0:T(1,128)}, bf16[128,2048]{1,0:T(8,128)(2,1)}, f32[1,129]{1,0:T(1,128)}, f32[128,2048]{1,0:T(8,128)}, /*index=5*/bf16[128,2048]{1,0:T(8,128)(2,1)}) custom-call(s32[1]{0:T(128)S(6)} %copy.14.offset_ref, bf16[256,512]{1,0:T(8,128)(2,1)} %get-tuple-element.15.route_ref, ...), custom_call_target="tpu_custom_call" | custom-call | tf_op jit(solution)/shard_map/pallas_call | solution.py:389
